TPU v7x, 32 devices: a whole 2x2x4 slice. The times are simulated.
32 devices in a mesh: section: 2 (over core), ctx: 4 (over z), tensor: 4 (over y, x).
Axes of the slice: x: 2, y: 2, z: 4, core: 2. Of those that a mesh axis runs over, the one named last changes fastest.
Arguments:
- boundary_in: bfloat16 [2, 4, 1024, 768], P('section', None, 'ctx'), may hold values from -6 to 6
- segments: int32 [4, 1024], replicated, may hold values from 0 to 2, never falling along the last dimension, each value on 1 to 512 neighbouring positions
- ln1_gain: bfloat16 [2, 768], P('section', 'ctx'), may hold values from 0.5 to 1.5
- ln1_bias: bfloat16 [2, 768], P('section', 'ctx'), may hold values from -2 to 2
- w_qkv: bfloat16 [2, 3, 768, 768], P('section', None, 'ctx', 'tensor'), may hold values from -0.21875 to 0.21875
- b_qv: bfloat16 [2, 2, 768], P('section', None, 'tensor'), may hold values from -0.29882812 to 0.29882812
- w_out: bfloat16 [2, 768, 768], P('section', 'tensor', 'ctx'), may hold values from -3 to 3
- b_out: bfloat16 [2, 768], P('section', 'ctx'), may hold values from -3 to 3
- ln2_gain: bfloat16 [2, 768], P('section', 'ctx'), may hold values from 0.5 to 1.5
- ln2_bias: bfloat16 [2, 768], P('section', 'ctx'), may hold values from -2 to 2
- w_up: bfloat16 [2, 768, 3072], P('section', 'ctx', 'tensor'), may hold values from -0.21875 to 0.21875
- b_up: bfloat16 [2, 3072], P('section', 'tensor'), may hold values from -3 to 3
- w_down: bfloat16 [2, 3072, 768], P('section', 'tensor', 'ctx'), may hold values from -0.109375 to 0.109375
- b_down: bfloat16 [2, 768], P('section', 'ctx'), may hold values from -2 to 2
Outputs:
- boundary_out: float32 [2, 4, 1024, 768], P('section', None, 'ctx')
- g_ln1_gain: float32 [2, 768], P('section', 'ctx')
- g_ln1_bias: float32 [2, 768], P('section', 'ctx')
- g_w_qkv: float32 [2, 3, 768, 768], P('section', None, 'ctx', 'tensor')
- g_b_qv: float32 [2, 2, 768], P('section', None, 'tensor')
- g_w_out: float32 [2, 768, 768], P('section', 'tensor', 'ctx')
- g_b_out: float32 [2, 768], P('section', 'ctx')
- g_ln2_gain: float32 [2, 768], P('section', 'ctx')
- g_ln2_bias: float32 [2, 768], P('section', 'ctx')
- g_w_up: float32 [2, 768, 3072], P('section', 'ctx', 'tensor')
- g_b_up: float32 [2, 3072], P('section', 'tensor')
- g_w_down: float32 [2, 3072, 768], P('section', 'tensor', 'ctx')
- g_b_down: float32 [2, 768], P('section', 'ctx')
Inputs may be any that keep to these rules, and one draw needn't show every extreme that they name: `segments`: document numbers never fall along a sequence; every document has 1 to 512 tokens, and one has exactly 512.
All inputs are finite; a program needn't handle non-finite values.
Results may differ from a plain program's by a relative error of at most 0.03.
Values may be sent and summed in bfloat16 or wider, within the bound.
A program may use at most 192 MiB of HBM per device.

v0:
```python
import math

import jax
import jax.numpy as jnp
from jax import lax
from jax.sharding import PartitionSpec as P

HEAD = 64


neg_big = -1e30
norm_eps = 1e-05


def taken_in(shard, axis, dim, absorb, state):
    everything = jax.tree.map(lambda a: lax.all_gather(a, axis, axis=dim, tiled=True), shard)
    return absorb(state, everything, jnp.int32(0))


def from_behind(value, axis, steps):
    count = lax.axis_size(axis)
    initial, last = (max(0, -steps), min(count, count - steps))
    return lax.ppermute(value, axis, [(source, source + steps) for source in range(initial, last)])


def smooth_act(values_in):
    return jax.nn.gelu(values_in, approximate=True)


def smooth_back(raised, grad_active):
    unused, pull = jax.vjp(smooth_act, raised)
    return pull(grad_active)[0]


def norm_parts(values_in, gain_vec, offset):
    average = jnp.mean(values_in, axis=-1, keepdims=True)
    centered = values_in - average
    inverse = lax.rsqrt(jnp.mean(centered * centered, axis=-1, keepdims=True) + norm_eps)
    normal = centered * inverse
    return (normal * gain_vec + offset, normal, inverse)


def norm_back(upstream, normal, inverse, gain_vec):
    scaled = upstream * gain_vec
    inner = (
        scaled
        - jnp.mean(scaled, axis=-1, keepdims=True)
        - normal * jnp.mean(scaled * normal, axis=-1, keepdims=True)
    )
    return (inner * inverse, jnp.sum(upstream * normal, axis=0), jnp.sum(upstream, axis=0))


def block_mask(seg_full, seg_rows, positions, first_key, key_count):
    key_seg = lax.dynamic_slice_in_dim(seg_full, first_key, key_count)
    key_pos = first_key + jnp.arange(key_count, dtype=jnp.int32)
    return (seg_rows[:, None] == key_seg[None, :]) & (key_pos[None, :] <= positions[:, None])


def fetch(shards):
    return (
        lax.all_gather(shards[0], "ctx", axis=0, tiled=True),
        lax.all_gather(shards[1], "ctx", axis=0, tiled=True),
        lax.all_gather(shards[2], "ctx", axis=1, tiled=True),
        lax.all_gather(shards[3], "ctx", axis=1, tiled=True),
        lax.all_gather(shards[4], "ctx", axis=0, tiled=True),
        lax.all_gather(shards[5], "ctx", axis=0, tiled=True),
        lax.all_gather(shards[6], "ctx", axis=0, tiled=True),
        lax.all_gather(shards[7], "ctx", axis=0, tiled=True),
        lax.all_gather(shards[8], "ctx", axis=1, tiled=True),
        lax.all_gather(shards[9], "ctx", axis=0, tiled=True),
    )


def branch_sum(partial_value):
    return lax.psum(partial_value.astype(jnp.bfloat16), "tensor").astype(jnp.float32)


def grad_sum(partial_value):
    return lax.psum(partial_value.astype(jnp.bfloat16), "tensor").astype(jnp.float32)


def attend_forward(query_rows, key_rows, value_rows, seg_full, seg_rows, positions):
    row_count, width = query_rows.shape
    head_count = width // HEAD
    query_h = query_rows.reshape(row_count, head_count, HEAD)
    totals_list = []

    def block_scores(key_block, first_key):
        key_count = key_block.shape[0]
        scores = jnp.einsum(
            "qhd,khd->hqk",
            query_h,
            key_block.reshape(key_count, head_count, HEAD),
            preferred_element_type=jnp.float32,
        )
        allowed = block_mask(seg_full, seg_rows, positions, first_key, key_count)[None]
        return (jnp.where(allowed, scores, neg_big), allowed)

    def first_fold(carried, pieces, first_key):
        key_block, value_block = pieces
        key_count = key_block.shape[0]
        row_max, row_sum = carried
        scores, allowed = block_scores(key_block, first_key)
        new_max = jnp.maximum(row_max, jnp.max(scores, axis=-1))
        chances = jnp.where(allowed, jnp.exp(scores - new_max[:, :, None]), 0.0)
        row_sum = jnp.sum(chances, axis=-1)
        return (new_max, row_sum)

    def second_fold(carried, pieces, first_key):
        key_block, value_block = pieces
        key_count = key_block.shape[0]
        scores, allowed = block_scores(key_block, first_key)
        weights_low = jnp.where(allowed, jnp.exp(scores - totals_list[0][:, :, None]), 0.0).astype(
            jnp.bfloat16
        )
        return jnp.einsum(
            "hqk,khd->hqd",
            weights_low,
            value_block.reshape(key_count, head_count, HEAD),
            preferred_element_type=jnp.float32,
        )

    folds = (first_fold, second_fold)
    starts = (
        (
            jnp.full((head_count, row_count), neg_big, jnp.float32),
            jnp.zeros((head_count, row_count), jnp.float32),
        ),
        jnp.zeros((head_count, row_count, HEAD), jnp.float32),
    )
    weighted = None
    for sweep in range(2):
        folded = taken_in((key_rows, value_rows), "ctx", 0, folds[sweep], starts[sweep])
        if sweep == 0:
            totals_list.append(folded[0] + jnp.log(folded[1]))
        else:
            weighted = folded
    return (jnp.transpose(weighted, (1, 0, 2)).reshape(row_count, width), totals_list[0])


def attend_backward(
    query_rows, grad_out, row_dot, log_total, key_all, value_all, seg_full, seg_rows, positions
):
    row_count, width = query_rows.shape
    head_count = width // HEAD
    query_h = query_rows.reshape(row_count, head_count, HEAD)
    grad_h = grad_out.reshape(row_count, head_count, HEAD)
    total_len = key_all.shape[0]
    block_len = min(512, total_len)
    block_count = total_len // block_len
    starts = jnp.arange(block_count, dtype=jnp.int32) * block_len

    def one_block(grad_query, members):
        key_block, value_block, first_key = members
        key_h = key_block.reshape(block_len, head_count, HEAD)
        value_h = value_block.reshape(block_len, head_count, HEAD)
        carried = grad_query
        scores = jnp.einsum("qhd,khd->hqk", query_h, key_h, preferred_element_type=jnp.float32)
        allowed = block_mask(seg_full, seg_rows, positions, first_key, block_len)[None]
        chances = jnp.where(allowed, jnp.exp(scores - log_total[:, :, None]), 0.0)
        grad_chance = jnp.einsum(
            "qhd,khd->hqk", grad_h, value_h, preferred_element_type=jnp.float32
        )
        grad_score = (chances * (grad_chance - row_dot[:, :, None])).astype(jnp.bfloat16)
        carried = carried + jnp.einsum(
            "hqk,khd->qhd", grad_score, key_h, preferred_element_type=jnp.float32
        )
        grad_value = jnp.einsum(
            "hqk,qhd->khd", chances.astype(jnp.bfloat16), grad_h, preferred_element_type=jnp.float32
        )
        grad_key = jnp.einsum(
            "hqk,qhd->khd", grad_score, query_h, preferred_element_type=jnp.float32
        )
        return (carried, (grad_key.reshape(block_len, width), grad_value.reshape(block_len, width)))

    grad_query, outputs = lax.scan(
        one_block,
        jnp.zeros((row_count, head_count, HEAD), jnp.float32),
        (
            key_all.reshape(block_count, block_len, width),
            value_all.reshape(block_count, block_len, width),
            starts,
        ),
    )
    return (
        grad_query.reshape(row_count, width),
        outputs[0].reshape(total_len, width),
        outputs[1].reshape(total_len, width),
    )


def layer_forward(values_in, gathered, bias_qv, bias_up, seg_full, seg_rows, positions):
    (
        gain_one,
        shift_one,
        proj_qkv,
        proj_out,
        bias_out,
        gain_two,
        shift_two,
        proj_up,
        proj_down,
        bias_down,
    ) = gathered
    normed, normal_one, inverse_one = norm_parts(
        values_in, gain_one.astype(jnp.float32), shift_one.astype(jnp.float32)
    )
    normed = normed.astype(jnp.bfloat16)
    projected = jnp.einsum("td,cde->cte", normed, proj_qkv, preferred_element_type=jnp.float32)
    scale = 1.0 / math.sqrt(HEAD)
    query_rows = ((projected[0] + bias_qv[0]) * scale).astype(jnp.bfloat16)
    key_rows = projected[1].astype(jnp.bfloat16)
    value_rows = (projected[2] + bias_qv[1]).astype(jnp.bfloat16)
    attended, log_total = attend_forward(
        query_rows, key_rows, value_rows, seg_full, seg_rows, positions
    )
    attended_low = attended.astype(jnp.bfloat16)
    branch = branch_sum(
        jnp.dot(attended_low, proj_out, preferred_element_type=jnp.float32)
    ) + bias_out.astype(jnp.float32)
    middle = values_in + branch
    normed_two, normal_two, inverse_two = norm_parts(
        middle, gain_two.astype(jnp.float32), shift_two.astype(jnp.float32)
    )
    normed_two = normed_two.astype(jnp.bfloat16)
    raised = jnp.dot(normed_two, proj_up, preferred_element_type=jnp.float32) + bias_up
    active = smooth_act(raised).astype(jnp.bfloat16)
    lowered = branch_sum(
        jnp.dot(active, proj_down, preferred_element_type=jnp.float32)
    ) + bias_down.astype(jnp.float32)
    saved = (
        normal_one,
        inverse_one,
        normed,
        query_rows,
        key_rows,
        value_rows,
        attended,
        attended_low,
        log_total,
        normal_two,
        inverse_two,
        normed_two,
        raised,
        active,
    )
    return (middle + lowered, saved)


def layer_backward(upstream, gathered, saved, seg_full, seg_rows, positions):
    (
        gain_one,
        shift_one,
        proj_qkv,
        proj_out,
        bias_out,
        gain_two,
        shift_two,
        proj_up,
        proj_down,
        bias_down,
    ) = gathered
    (
        normal_one,
        inverse_one,
        normed,
        query_rows,
        key_rows,
        value_rows,
        attended,
        attended_low,
        log_total,
        normal_two,
        inverse_two,
        normed_two,
        raised,
        active,
    ) = saved
    upstream_low = upstream.astype(jnp.bfloat16)
    grad_bias_down = jnp.sum(upstream_low.astype(jnp.float32), axis=0)
    grad_proj_down = jnp.einsum(
        "tf,td->fd", active, upstream_low, preferred_element_type=jnp.float32
    )
    grad_active = jnp.einsum(
        "td,fd->tf", upstream_low, proj_down, preferred_element_type=jnp.float32
    )
    grad_raised = smooth_back(raised, grad_active).astype(jnp.bfloat16)
    grad_bias_up = jnp.sum(grad_raised.astype(jnp.float32), axis=0)
    grad_proj_up = jnp.einsum(
        "td,tf->df", normed_two, grad_raised, preferred_element_type=jnp.float32
    )
    grad_normed_two = grad_sum(
        jnp.einsum("tf,df->td", grad_raised, proj_up, preferred_element_type=jnp.float32)
    )
    grad_mid_norm, grad_gain_two, grad_shift_two = norm_back(
        grad_normed_two, normal_two, inverse_two, gain_two.astype(jnp.float32)
    )
    grad_middle = upstream + grad_mid_norm
    grad_branch = grad_middle.astype(jnp.bfloat16)
    grad_bias_out = jnp.sum(grad_branch.astype(jnp.float32), axis=0)
    grad_proj_out = jnp.einsum(
        "te,td->ed", attended_low, grad_branch, preferred_element_type=jnp.float32
    )
    grad_attended = jnp.einsum(
        "td,ed->te", grad_branch, proj_out, preferred_element_type=jnp.float32
    ).astype(jnp.bfloat16)
    row_count, width = query_rows.shape
    head_count = width // HEAD
    row_dot = jnp.transpose(
        jnp.sum(
            (grad_attended.astype(jnp.float32) * attended).reshape(row_count, head_count, HEAD),
            axis=-1,
        )
    )
    key_all, value_all = (
        lax.all_gather(key_rows, "ctx", axis=0, tiled=True),
        lax.all_gather(value_rows, "ctx", axis=0, tiled=True),
    )
    grad_query, grad_keys, grad_values = attend_backward(
        query_rows,
        grad_attended,
        row_dot,
        log_total,
        key_all,
        value_all,
        seg_full,
        seg_rows,
        positions,
    )
    own_keys, own_values = (
        lax.psum_scatter(
            grad_keys.astype(jnp.bfloat16), "ctx", scatter_dimension=0, tiled=True
        ).astype(jnp.float32),
        lax.psum_scatter(
            grad_values.astype(jnp.bfloat16), "ctx", scatter_dimension=0, tiled=True
        ).astype(jnp.float32),
    )
    scale = 1.0 / math.sqrt(HEAD)
    query_low = grad_query.astype(jnp.bfloat16).astype(jnp.float32) * scale
    value_low = own_values.astype(jnp.bfloat16)
    grad_projected = jnp.stack(
        [query_low.astype(jnp.bfloat16), own_keys.astype(jnp.bfloat16), value_low]
    )
    grad_bias_qv = jnp.stack(
        [jnp.sum(query_low, axis=0), jnp.sum(value_low.astype(jnp.float32), axis=0)]
    )
    grad_proj_qkv = jnp.einsum(
        "td,cte->cde", normed, grad_projected, preferred_element_type=jnp.float32
    )
    grad_normed = grad_sum(
        jnp.einsum("cte,cde->td", grad_projected, proj_qkv, preferred_element_type=jnp.float32)
    )
    grad_in_norm, grad_gain_one, grad_shift_one = norm_back(
        grad_normed, normal_one, inverse_one, gain_one.astype(jnp.float32)
    )
    main_grads = (
        grad_gain_one,
        grad_shift_one,
        grad_proj_qkv,
        grad_proj_out,
        grad_bias_out,
        grad_gain_two,
        grad_shift_two,
        grad_proj_up,
        grad_proj_down,
        grad_bias_down,
    )
    return (grad_middle + grad_in_norm, main_grads, (grad_bias_qv, grad_bias_up))


def local(
    boundary_in,
    segments,
    ln1_gain,
    ln1_bias,
    w_qkv,
    b_qv,
    w_out,
    b_out,
    ln2_gain,
    ln2_bias,
    w_up,
    b_up,
    w_down,
    b_down,
):
    section_id = lax.axis_index("section")
    ctx_id = lax.axis_index("ctx")
    micro = boundary_in.shape[1]
    row_count = boundary_in.shape[2]
    width = boundary_in.shape[3]
    shards = (
        ln1_gain[0],
        ln1_bias[0],
        w_qkv[0],
        w_out[0],
        b_out[0],
        ln2_gain[0],
        ln2_bias[0],
        w_up[0],
        w_down[0],
        b_down[0],
    )
    bias_qv = b_qv[0].astype(jnp.float32)
    bias_up = b_up[0].astype(jnp.float32)
    positions = ctx_id * row_count + jnp.arange(row_count, dtype=jnp.int32)
    received = jnp.zeros((row_count, width), jnp.bfloat16)
    saved_list = []
    results = []
    for micro_step in range(micro + 1):
        gathered = fetch(shards)
        batch_index = jnp.clip(micro_step - section_id, 0, micro - 1)
        seg_full = lax.dynamic_index_in_dim(segments, batch_index, 0, keepdims=False)
        seg_rows = lax.dynamic_slice_in_dim(seg_full, ctx_id * row_count, row_count)
        source = jnp.where(section_id == 0, boundary_in[0, min(micro_step, micro - 1)], received)
        result, saved = layer_forward(
            source.astype(jnp.float32), gathered, bias_qv, bias_up, seg_full, seg_rows, positions
        )
        received = from_behind(result.astype(jnp.bfloat16), "section", 1)
        saved_list.append(saved)
        results.append(result)
    stacked = jax.tree.map(lambda *members: jnp.stack(members), *saved_list)
    returned = jnp.zeros((row_count, width), jnp.bfloat16)
    input_grads = []
    main_sums = None
    small_sums = None
    for micro_step in range(micro + 1):
        gathered = fetch(shards)
        chosen = micro_step - 1 + section_id
        usable = (chosen >= 0) & (chosen < micro)
        batch_index = jnp.clip(chosen, 0, micro - 1)
        seg_full = lax.dynamic_index_in_dim(segments, batch_index, 0, keepdims=False)
        seg_rows = lax.dynamic_slice_in_dim(seg_full, ctx_id * row_count, row_count)
        forward_step = jnp.clip(chosen + section_id, 0, micro)
        saved = jax.tree.map(
            lambda member: lax.dynamic_index_in_dim(member, forward_step, 0, keepdims=False),
            stacked,
        )
        incoming = jnp.where(section_id == 1, boundary_in[0, min(micro_step, micro - 1)], returned)
        grad_input, main_grads, small_grads = layer_backward(
            incoming.astype(jnp.float32), gathered, saved, seg_full, seg_rows, positions
        )
        returned = from_behind(grad_input.astype(jnp.bfloat16), "section", -1)
        main_grads = jax.tree.map(lambda member: jnp.where(usable, member, 0.0), main_grads)
        small_grads = jax.tree.map(lambda member: jnp.where(usable, member, 0.0), small_grads)
        if main_sums is None:
            main_sums = main_grads
            small_sums = small_grads
        else:
            main_sums = jax.tree.map(jnp.add, main_sums, main_grads)
            small_sums = jax.tree.map(jnp.add, small_sums, small_grads)
        input_grads.append(grad_input)
    owned = (
        lax.psum_scatter(
            main_sums[0].astype(jnp.bfloat16), "ctx", scatter_dimension=0, tiled=True
        ).astype(jnp.float32),
        lax.psum_scatter(
            main_sums[1].astype(jnp.bfloat16), "ctx", scatter_dimension=0, tiled=True
        ).astype(jnp.float32),
        lax.psum_scatter(
            main_sums[2].astype(jnp.bfloat16), "ctx", scatter_dimension=1, tiled=True
        ).astype(jnp.float32),
        lax.psum_scatter(
            main_sums[3].astype(jnp.bfloat16), "ctx", scatter_dimension=1, tiled=True
        ).astype(jnp.float32),
        lax.psum_scatter(
            main_sums[4].astype(jnp.bfloat16), "ctx", scatter_dimension=0, tiled=True
        ).astype(jnp.float32),
        lax.psum_scatter(
            main_sums[5].astype(jnp.bfloat16), "ctx", scatter_dimension=0, tiled=True
        ).astype(jnp.float32),
        lax.psum_scatter(
            main_sums[6].astype(jnp.bfloat16), "ctx", scatter_dimension=0, tiled=True
        ).astype(jnp.float32),
        lax.psum_scatter(
            main_sums[7].astype(jnp.bfloat16), "ctx", scatter_dimension=0, tiled=True
        ).astype(jnp.float32),
        lax.psum_scatter(
            main_sums[8].astype(jnp.bfloat16), "ctx", scatter_dimension=1, tiled=True
        ).astype(jnp.float32),
        lax.psum_scatter(
            main_sums[9].astype(jnp.bfloat16), "ctx", scatter_dimension=0, tiled=True
        ).astype(jnp.float32),
    )
    bias_totals = lax.psum((small_sums[0], small_sums[1]), "ctx")
    ends = jnp.where(section_id == 0, jnp.stack(input_grads[1:]), jnp.stack(results[1:]))
    return (
        ends[None],
        owned[0][None],
        owned[1][None],
        owned[2][None],
        bias_totals[0][None],
        owned[3][None],
        owned[4][None],
        owned[5][None],
        owned[6][None],
        owned[7][None],
        bias_totals[1][None],
        owned[8][None],
        owned[9][None],
    )


def solution(mesh):
    in_specs = (
        P("section", None, "ctx", None),
        P(),
        P("section", "ctx"),
        P("section", "ctx"),
        P("section", None, "ctx", "tensor"),
        P("section", None, "tensor"),
        P("section", "tensor", "ctx"),
        P("section", "ctx"),
        P("section", "ctx"),
        P("section", "ctx"),
        P("section", "ctx", "tensor"),
        P("section", "tensor"),
        P("section", "tensor", "ctx"),
        P("section", "ctx"),
    )
    out_specs = (
        P("section", None, "ctx", None),
        P("section", "ctx"),
        P("section", "ctx"),
        P("section", None, "ctx", "tensor"),
        P("section", None, "tensor"),
        P("section", "tensor", "ctx"),
        P("section", "ctx"),
        P("section", "ctx"),
        P("section", "ctx"),
        P("section", "ctx", "tensor"),
        P("section", "tensor"),
        P("section", "tensor", "ctx"),
        P("section", "ctx"),
    )
    return jax.shard_map(local, mesh=mesh, in_specs=in_specs, out_specs=out_specs, check_vma=False)
```

profile of v0, /device:TPU:0, one launch (start us, length us, event | category | flops | bytes accessed | tf_op | source)
XLA Modules:
  0.0 1729.8 jit_solution(7897125028865360060)
XLA Ops:
  13.8 31.7 %all-gather.3 = bf16[1,3,768,192]{3,1,0,2:T(4,128)(2,1)} all-gather(bf16[1,3,192,192]{3,1,0,2:T(4,128)(2,1)S(1)} %copy.173), channel_id=5, replica_groups=mesh['section'=2,'ctx'=4,'tensor'=4] {'ctx'}, dimensions={2}, use_global_device_ids=true | all-gather | bytes 1105920 | tf_op jit(solution)/shard_map/all_gather | solution.py:63
  50.9 19.8 %all-reduce.15 = (bf16[768]{0:T(1024)(128)(2,1)S(1)}, bf16[768]{0:T(1024)(128)(2,1)S(1)}, bf16[768]{0:T(1024)(128)(2,1)S(1)}, bf16[768]{0:T(1024)(128)(2,1)}, bf...) all-reduce(bf16[768]{0:T(1024)(128)(2,1)S(1)} %dynamic-update-slice, ...), channel_id=4, replica_groups=mesh['section'=2,'ctx'=4,'tensor'=4] {'ctx'}, use_global_device_ids=true, to_apply=%add.1 | all-reduce | flops 4608 | bytes 18432
  71.4 15.9 all_gather.65
  88.8 14.3 all-gather.4
  110.7 15.7 all-gather.5
  126.9 3.7 bitcast_convert_fusion.12
  132.9 41.4 %all-reduce.36.cloned.1.call-done = bf16[256,768]{1,0:T(8,128)(2,1)} async-done(((bf16[256,768]{1,0:T(8,128)(2,1)}), bf16[256,768]{1,0:T(8,128)(2,1)}) %all-reduce.36.cloned.1.call-update) | async-done | bytes 393232 | tf_op jit(solution)/shard_map/psum | solution.py:75
  180.5 12.9 all-gather.28.cloned.1.call-done
  196.1 43.4 %all-reduce.38.cloned.1.call-done = bf16[256,768]{1,0:T(8,128)(2,1)} async-done(((bf16[256,768]{1,0:T(8,128)(2,1)}), bf16[256,768]{1,0:T(8,128)(2,1)}) %all-reduce.38.cloned.1.call-update) | async-done | bytes 393232 | tf_op jit(solution)/shard_map/psum | solution.py:75
  245.7 14.8 all_gather.73
  261.3 15.7 all-gather.11
  282.4 44.1 %all-reduce.40.cloned.1.call-done = bf16[256,768]{1,0:T(8,128)(2,1)} async-done(((bf16[256,768]{1,0:T(8,128)(2,1)}), bf16[256,768]{1,0:T(8,128)(2,1)}) %all-reduce.40.cloned.1.call-update) | async-done | bytes 393232 | tf_op jit(solution)/shard_map/psum | solution.py:75
  334.0 44.2 %all-reduce.42.cloned.1.call-done = bf16[256,768]{1,0:T(8,128)(2,1)} async-done(((bf16[256,768]{1,0:T(8,128)(2,1)}), bf16[256,768]{1,0:T(8,128)(2,1)}) %all-reduce.42.cloned.1.call-update) | async-done | bytes 393232 | tf_op jit(solution)/shard_map/psum | solution.py:75
  384.5 14.7 all_gather.75
  400.1 15.2 all-gather.12
  420.8 44.0 %all-reduce.44.cloned.1.call-done = bf16[256,768]{1,0:T(8,128)(2,1)} async-done(((bf16[256,768]{1,0:T(8,128)(2,1)}), bf16[256,768]{1,0:T(8,128)(2,1)}) %all-reduce.44.cloned.1.call-update) | async-done | bytes 393232 | tf_op jit(solution)/shard_map/psum | solution.py:75
  474.9 42.0 %all-reduce.46.cloned.1.call-done = bf16[256,768]{1,0:T(8,128)(2,1)} async-done(((bf16[256,768]{1,0:T(8,128)(2,1)}), bf16[256,768]{1,0:T(8,128)(2,1)}) %all-reduce.46.cloned.1.call-update) | async-done | bytes 393232 | tf_op jit(solution)/shard_map/psum | solution.py:75
  524.9 14.5 all_gather.77
  540.2 15.2 all-gather.13
  566.4 38.9 %all-reduce.48.cloned.1.call-done = bf16[256,768]{1,0:T(8,128)(2,1)} async-done(((bf16[256,768]{1,0:T(8,128)(2,1)}), bf16[256,768]{1,0:T(8,128)(2,1)}) %all-reduce.48.cloned.1.call-update) | async-done | bytes 393232 | tf_op jit(solution)/shard_map/psum | solution.py:75
  617.5 39.7 %all-reduce.50.cloned.1.call-done = bf16[256,768]{1,0:T(8,128)(2,1)} async-done(((bf16[256,768]{1,0:T(8,128)(2,1)}), bf16[256,768]{1,0:T(8,128)(2,1)}) %all-reduce.50.cloned.1.call-update) | async-done | bytes 393232 | tf_op jit(solution)/shard_map/psum | solution.py:75
  664.2 14.6 all_gather.79
  679.7 15.3 all-gather.14
  702.5 16.0 all-gather.15
  720.4 14.9 all-gather.16
  764.5 38.6 %all-reduce.54.cloned.1.call-done = bf16[256,768]{1,0:T(8,128)(2,1)} async-done(((bf16[256,768]{1,0:T(8,128)(2,1)}), bf16[256,768]{1,0:T(8,128)(2,1)}) %all-reduce.54.cloned.1.call-update) | async-done | bytes 393232 | tf_op jit(solution)/shard_map/psum | solution.py:79
  811.8 23.4 %while.75 = (s32[]{:T(128)}, f32[256,3,64]{0,2,1:T(8,128)}, bf16[2,512,192]{1,2,0:T(8,128)(2,1)}, bf16[2,512,192]{1,2,0:T(8,128)(2,1)}, bf16[2,512,192]{1,2,0:T(...) while((s32[]{:T(128)}, f32[256,3,64]{0,2,1:T(8,128)}, ...), condition=%wide.region_44.45_spmd.clone, body=%wide.region_43.44_spmd.clone.sunk | while | flops 254509824 | bytes 17005952 | solution.py:176
  839.7 18.1 %reduce-scatter.23.cloned.1.call-done = bf16[256,192]{0,1:T(8,128)(2,1)} async-done(((bf16[1024,192]{0,1:T(8,128)(2,1)}), bf16[256,192]{0,1:T(8,128)(2,1)}) %reduce-scatter.23.cloned.1.call-update) | async-done | bytes 98320 | tf_op jit(solution)/shard_map/reduce_scatter | solution.py:334
  857.8 21.7 %reduce-scatter.21.cloned.1.call-done = bf16[256,192]{0,1:T(8,128)(2,1)} async-done(((bf16[1024,192]{0,1:T(8,128)(2,1)}), bf16[256,192]{0,1:T(8,128)(2,1)}) %reduce-scatter.21.cloned.1.call-update) | async-done | bytes 98320 | tf_op jit(solution)/shard_map/reduce_scatter | solution.py:331
  881.8 42.3 %all-reduce.56.cloned.1.call-done = bf16[256,768]{1,0:T(8,128)(2,1)} async-done(((bf16[256,768]{1,0:T(8,128)(2,1)}), bf16[256,768]{1,0:T(8,128)(2,1)}) %all-reduce.56.cloned.1.call-update) | async-done | bytes 393232 | tf_op jit(solution)/shard_map/psum | solution.py:79
  937.3 14.7 all-gather.17
  953.0 15.9 all-gather.18
  970.0 11.4 all-reduce.58.cloned.1.call-done
  990.0 24.6 %while.76 = (s32[]{:T(128)}, f32[256,3,64]{0,2,1:T(8,128)}, bf16[2,512,192]{1,2,0:T(8,128)(2,1)}, bf16[2,512,192]{1,2,0:T(8,128)(2,1)}, bf16[2,512,192]{1,2,0:T(...) while((s32[]{:T(128)}, f32[256,3,64]{0,2,1:T(8,128)}, ...), condition=%wide.region_55.56_spmd.clone, body=%wide.region_54.55_spmd.clone.sunk | while | flops 254509824 | bytes 17005952 | solution.py:176
  1019.2 18.1 %reduce-scatter.27.cloned.1.call-done = bf16[256,192]{0,1:T(8,128)(2,1)} async-done(((bf16[1024,192]{0,1:T(8,128)(2,1)}), bf16[256,192]{0,1:T(8,128)(2,1)}) %reduce-scatter.27.cloned.1.call-update) | async-done | bytes 98320 | tf_op jit(solution)/shard_map/reduce_scatter | solution.py:334
  1037.2 21.7 %reduce-scatter.25.cloned.1.call-done = bf16[256,192]{0,1:T(8,128)(2,1)} async-done(((bf16[1024,192]{0,1:T(8,128)(2,1)}), bf16[256,192]{0,1:T(8,128)(2,1)}) %reduce-scatter.25.cloned.1.call-update) | async-done | bytes 98320 | tf_op jit(solution)/shard_map/reduce_scatter | solution.py:331
  1061.3 42.2 %all-reduce.60.cloned.1.call-done = bf16[256,768]{1,0:T(8,128)(2,1)} async-done(((bf16[256,768]{1,0:T(8,128)(2,1)}), bf16[256,768]{1,0:T(8,128)(2,1)}) %all-reduce.60.cloned.1.call-update) | async-done | bytes 393232 | tf_op jit(solution)/shard_map/psum | solution.py:79
  1117.6 14.7 all-gather.19
  1133.4 15.5 all-gather.20
  1150.0 11.8 all-reduce.62.cloned.1.call-done
  1170.4 23.5 %while.77 = (s32[]{:T(128)}, f32[256,3,64]{0,2,1:T(8,128)}, bf16[2,512,192]{1,2,0:T(8,128)(2,1)}, bf16[2,512,192]{1,2,0:T(8,128)(2,1)}, bf16[2,512,192]{1,2,0:T(...) while((s32[]{:T(128)}, f32[256,3,64]{0,2,1:T(8,128)}, ...), condition=%wide.region_66.67_spmd.clone, body=%wide.region_65.66_spmd.clone.sunk | while | flops 254509824 | bytes 17005952 | solution.py:176
  1198.4 18.0 %reduce-scatter.31.cloned.1.call-done = bf16[256,192]{0,1:T(8,128)(2,1)} async-done(((bf16[1024,192]{0,1:T(8,128)(2,1)}), bf16[256,192]{0,1:T(8,128)(2,1)}) %reduce-scatter.31.cloned.1.call-update) | async-done | bytes 98320 | tf_op jit(solution)/shard_map/reduce_scatter | solution.py:334
  1216.4 21.5 %reduce-scatter.29.cloned.1.call-done = bf16[256,192]{0,1:T(8,128)(2,1)} async-done(((bf16[1024,192]{0,1:T(8,128)(2,1)}), bf16[256,192]{0,1:T(8,128)(2,1)}) %reduce-scatter.29.cloned.1.call-update) | async-done | bytes 98320 | tf_op jit(solution)/shard_map/reduce_scatter | solution.py:331
  1241.7 40.8 %all-reduce.64.cloned.1.call-done = bf16[256,768]{1,0:T(8,128)(2,1)} async-done(((bf16[256,768]{1,0:T(8,128)(2,1)}), bf16[256,768]{1,0:T(8,128)(2,1)}) %all-reduce.64.cloned.1.call-update) | async-done | bytes 393232 | tf_op jit(solution)/shard_map/psum | solution.py:79
  1296.7 15.2 all-gather.21
  1313.0 14.4 all-gather.22
  1328.5 12.5 all-reduce.66.cloned.1.call-done
  1349.6 24.3 %while.78 = (s32[]{:T(128)}, f32[256,3,64]{0,2,1:T(8,128)}, bf16[2,512,192]{1,2,0:T(8,128)(2,1)}, bf16[2,512,192]{1,2,0:T(8,128)(2,1)}, bf16[2,512,192]{1,2,0:T(...) while((s32[]{:T(128)}, f32[256,3,64]{0,2,1:T(8,128)}, ...), condition=%wide.region_77.78_spmd.clone, body=%wide.region_76.77_spmd.clone.sunk | while | flops 254509824 | bytes 17005952 | solution.py:176
  1386.2 10.5 reduce-scatter.35.cloned.1.call-done
  1396.6 21.7 %reduce-scatter.33.cloned.1.call-done = bf16[256,192]{0,1:T(8,128)(2,1)} async-done(((bf16[1024,192]{0,1:T(8,128)(2,1)}), bf16[256,192]{0,1:T(8,128)(2,1)}) %reduce-scatter.33.cloned.1.call-update) | async-done | bytes 98320 | tf_op jit(solution)/shard_map/reduce_scatter | solution.py:331
  1421.7 14.4 all-gather.23
  1437.1 25.8 %all-reduce.68.cloned.1.call-done = bf16[256,768]{1,0:T(8,128)(2,1)} async-done(((bf16[256,768]{1,0:T(8,128)(2,1)}), bf16[256,768]{1,0:T(8,128)(2,1)}) %all-reduce.68.cloned.1.call-update) | async-done | bytes 393232 | tf_op jit(solution)/shard_map/psum | solution.py:79
  1468.9 15.4 all-gather.24
  1498.9 39.2 %all-reduce.70.cloned.1.call-done = bf16[256,768]{1,0:T(8,128)(2,1)} async-done(((bf16[256,768]{1,0:T(8,128)(2,1)}), bf16[256,768]{1,0:T(8,128)(2,1)}) %all-reduce.70.cloned.1.call-update) | async-done | bytes 393232 | tf_op jit(solution)/shard_map/psum | solution.py:79
  1546.0 20.3 %while.79 = (s32[]{:T(128)}, f32[256,3,64]{0,2,1:T(8,128)S(1)}, bf16[2,512,192]{1,2,0:T(8,128)(2,1)}, bf16[2,512,192]{1,2,0:T(8,128)(2,1)}, bf16[2,512,192]{1,2,...) while((s32[]{:T(128)}, f32[256,3,64]{0,2,1:T(8,128)S(1)}, ...), condition=%wide.region_88.89_spmd.clone, body=%wide.region_87.88_spmd.clone.sunk | while | flops 254509824 | bytes 17005952 | solution.py:176
  1584.2 4.7 reduce-scatter.39.cloned.1.call-done
  1588.9 21.6 %reduce-scatter.37.cloned.1.call-done = bf16[256,192]{0,1:T(8,128)(2,1)} async-done(((bf16[1024,192]{0,1:T(8,128)(2,1)}), bf16[256,192]{0,1:T(8,128)(2,1)}) %reduce-scatter.37.cloned.1.call-update) | async-done | bytes 98320 | tf_op jit(solution)/shard_map/reduce_scatter | solution.py:331
  1614.4 3.7 add_convert_fusion
  1638.1 4.7 add_convert_fusion.1
  1651.0 3.6 fusion.40
  1656.8 4.1 reshape.2070
  1661.1 9.1 all-reduce.12
  1671.9 18.7 %all-reduce.14 = (bf16[768]{0:T(1024)(128)(2,1)S(1)}, bf16[768]{0:T(1024)(128)(2,1)S(1)}, bf16[768]{0:T(1024)(128)(2,1)S(1)}, bf16[768]{0:T(1024)(128)(2,1)S(1)}...) all-reduce(bf16[768]{0:T(1024)(128)(2,1)S(1)} %add_convert_fusion.1, ...), channel_id=37, replica_groups=mesh['section'=2,'ctx'=4,'tensor'=4] {'ctx'}, use_global_device_ids=true, to_apply=%region_100.101.clone | all-reduce | flops 4608 | bytes 18432
  1703.0 16.5 reduce-scatter.43.cloned.1.call-done
  (1225 shorter events, 464.1 us)
Async XLA Ops:
  8.0 166.4 %all-reduce.36.cloned.1.call-start = ((), (), s32[]{:S(2)}) async-start(), calls=%async_computation.14 | async-start | bytes 786432 | tf_op jit(solution)/shard_map/psum | solution.py:75
  9.4 78.6 %copy-start.174 = (f32[1,1,192]{2,1,0:T(1,128)}, f32[1,1,192]{2,1,0:T(1,128)S(1)}, u32[]{:S(2)}) copy-start(f32[1,1,192]{2,1,0:T(1,128)S(1)} %get-tuple-element.1336) | copy-start | bytes 2308
  9.4 251.1 %copy-start.160 = (f32[1,1,192]{2,1,0:T(1,128)}, f32[1,1,192]{2,1,0:T(1,128)S(1)}, u32[]{:S(2)}) copy-start(f32[1,1,192]{2,1,0:T(1,128)S(1)} %get-tuple-element.1337) | copy-start | bytes 2308
  11.3 59.5 %copy-start.246 = (f32[256]{0:T(256)}, f32[256]{0:T(256)S(1)}, u32[]{:S(2)}) copy-start(f32[256]{0:T(256)S(1)} %broadcast_multiply_fusion.29) | copy-start | bytes 3076
  12.5 58.2 %copy-start.252 = (f32[256]{0:T(256)}, f32[256]{0:T(256)S(1)}, u32[]{:S(2)}) copy-start(f32[256]{0:T(256)S(1)} %add_rsqrt_fusion.9) | copy-start | bytes 3076
  13.8 56.9 %copy-start.5 = (bf16[1,4,256,768]{3,2,1,0:T(8,128)(2,1)S(1)}, bf16[1,4,256,768]{3,2,1,0:T(8,128)(2,1)}, u32[]{:S(2)}) copy-start(bf16[1,4,256,768]{3,2,1,0:T(8,128)(2,1)} %param.24) | copy-start | bytes 4718596
  70.7 313.0 %copy-start.146 = (f32[768]{0:T(1024)}, f32[768]{0:T(1024)S(1)}, u32[]{:S(2)}) copy-start(f32[768]{0:T(1024)S(1)} %convert_element_type.1173) | copy-start | bytes 9220
  103.2 173.8 %copy-start.170 = (f32[3,64]{1,0:T(4,128)}, f32[3,64]{1,0:T(4,128)S(1)}, u32[]{:S(2)}) copy-start(f32[3,64]{1,0:T(4,128)S(1)} %add.1142) | copy-start | bytes 2308
  131.6 46.0 %all-gather.30.cloned.1.call-start = ((), (), s32[]{:S(2)}) async-start(), calls=%async_computation.44 | async-start | bytes 1474560 | tf_op jit(solution)/shard_map/all_gather | solution.py:68
  132.2 61.2 %all-gather.28.cloned.1.call-start = ((), (), s32[]{:S(2)}) async-start(), calls=%async_computation.43 | async-start | bytes 1474560 | tf_op jit(solution)/shard_map/all_gather | solution.py:69
  132.8 106.7 %all-reduce.38.cloned.1.call-start = ((), (), s32[]{:S(2)}) async-start(), calls=%async_computation.15 | async-start | bytes 786432 | tf_op jit(solution)/shard_map/psum | solution.py:75
  132.9 196.2 %copy-start.149 = (f32[768]{0:T(1024)}, f32[768]{0:T(1024)S(1)}, u32[]{:S(2)}) copy-start(f32[768]{0:T(1024)S(1)} %convert_element_type.1176) | copy-start | bytes 9220
  132.9 196.1 %copy-start.272 = (f32[768]{0:T(1024)}, f32[768]{0:T(1024)S(1)}, u32[]{:S(2)}) copy-start(f32[768]{0:T(1024)S(1)} %convert_reduce_fusion.35) | copy-start | bytes 9220
  180.5 60.2 %copy-start.108 = (f32[256,768]{1,0:T(8,128)}, f32[256,768]{1,0:T(8,128)S(1)}, u32[]{:S(2)}) copy-start(f32[256,768]{1,0:T(8,128)S(1)} %get-tuple-element.1366) | copy-start | bytes 2359300
  180.5 59.0 %copy-start.38 = (bf16[256,768]{1,0:T(8,128)(2,1)S(1)}, bf16[256,768]{1,0:T(8,128)(2,1)}, u32[]{:S(2)}) copy-start(bf16[256,768]{1,0:T(8,128)(2,1)} %all-reduce.36.cloned.1.call-done) | copy-start | bytes 1179652
  196.0 130.5 %all-reduce.40.cloned.1.call-start = ((), (), s32[]{:S(2)}) async-start(), calls=%async_computation.16 | async-start | bytes 786432 | tf_op jit(solution)/shard_map/psum | solution.py:75
  196.1 461.1 %copy-start.144 = (f32[768]{0:T(1024)}, f32[768]{0:T(1024)S(1)}, u32[]{:S(2)}) copy-start(f32[768]{0:T(1024)S(1)} %convert_element_type.1177) | copy-start | bytes 9220
  240.7 2.6 collective-permute-start
  282.4 95.8 %all-reduce.42.cloned.1.call-start = ((), (), s32[]{:S(2)}) async-start(), calls=%async_computation.17 | async-start | bytes 786432 | tf_op jit(solution)/shard_map/psum | solution.py:75
  334.0 130.8 %all-reduce.44.cloned.1.call-start = ((), (), s32[]{:S(2)}) async-start(), calls=%async_computation.18 | async-start | bytes 786432 | tf_op jit(solution)/shard_map/psum | solution.py:75
  380.5 2.8 collective-permute-start.1
  420.7 96.1 %all-reduce.46.cloned.1.call-start = ((), (), s32[]{:S(2)}) async-start(), calls=%async_computation.19 | async-start | bytes 786432 | tf_op jit(solution)/shard_map/psum | solution.py:75
  472.6 48.3 %copy-start.256 = (f32[256]{0:T(256)S(1)}, f32[256]{0:T(256)}, u32[]{:S(2)}) copy-start(f32[256]{0:T(256)} %copy-done.255) | copy-start | bytes 3076
  472.6 132.6 %all-reduce.48.cloned.1.call-start = ((), (), s32[]{:S(2)}) async-start(), calls=%async_computation.20 | async-start | bytes 786432 | tf_op jit(solution)/shard_map/psum | solution.py:75
  519.2 4.4 collective-permute-start.2
  560.7 96.5 %all-reduce.50.cloned.1.call-start = ((), (), s32[]{:S(2)}) async-start(), calls=%async_computation.21 | async-start | bytes 786432 | tf_op jit(solution)/shard_map/psum | solution.py:75
  606.6 54.9 %copy-start.196 = (f32[256]{0:T(256)}, f32[256]{0:T(256)S(1)}, u32[]{:S(2)}) copy-start(f32[256]{0:T(256)S(1)} %broadcast_multiply_fusion.22) | copy-start | bytes 3076
  608.0 53.5 %copy-start.244 = (f32[256]{0:T(256)}, f32[256]{0:T(256)S(1)}, u32[]{:S(2)}) copy-start(f32[256]{0:T(256)S(1)} %add_rsqrt_fusion.2) | copy-start | bytes 3076
  613.0 136.0 %all-reduce.52.cloned.1.call-start = ((), (), s32[]{:S(2)}) async-start(), calls=%async_computation.22 | async-start | bytes 786432 | tf_op jit(solution)/shard_map/psum | solution.py:75
  659.6 3.4 collective-permute-start.3
  700.4 102.8 %all-reduce.54.cloned.1.call-start = ((), (), s32[]{:S(2)}) async-start(), calls=%async_computation.23 | async-start | bytes 786432 | tf_op jit(solution)/shard_map/psum | solution.py:79
  759.3 98.5 %reduce-scatter.23.cloned.1.call-start = ((), (), s32[]{:S(2)}) async-start(), calls=%async_computation.25 | async-start | bytes 491520 | tf_op jit(solution)/shard_map/reduce_scatter | solution.py:334
  837.1 42.4 %reduce-scatter.21.cloned.1.call-start = ((), (), s32[]{:S(2)}) async-start(), calls=%async_computation.24 | async-start | bytes 491520 | tf_op jit(solution)/shard_map/reduce_scatter | solution.py:331
  838.9 85.1 %all-reduce.56.cloned.1.call-start = ((), (), s32[]{:S(2)}) async-start(), calls=%async_computation.26 | async-start | bytes 786432 | tf_op jit(solution)/shard_map/psum | solution.py:79
  839.7 86.6 %copy-start.135 = (bf16[256,3,64]{0,2,1:T(8,128)(2,1)}, bf16[256,3,64]{0,2,1:T(8,128)(2,1)S(1)}, u32[]{:S(2)}) copy-start(bf16[256,3,64]{0,2,1:T(8,128)(2,1)S(1)} %get-tuple-element.1292) | copy-start | bytes 294916
  881.8 99.7 %all-reduce.58.cloned.1.call-start = ((), (), s32[]{:S(2)}) async-start(), calls=%async_computation.27 | async-start | bytes 786432 | tf_op jit(solution)/shard_map/psum | solution.py:79
  927.9 3.6 collective-permute-start.4
  933.2 50.4 %copy-start.49 = (bf16[256,768]{1,0:T(8,128)(2,1)}, bf16[256,768]{1,0:T(8,128)(2,1)S(1)}, u32[]{:S(2)}) copy-start(bf16[256,768]{1,0:T(8,128)(2,1)S(1)} %get-tuple-element.1169) | copy-start | bytes 1179652
  937.2 100.1 %reduce-scatter.27.cloned.1.call-start = ((), (), s32[]{:S(2)}) async-start(), calls=%async_computation.29 | async-start | bytes 491520 | tf_op jit(solution)/shard_map/reduce_scatter | solution.py:334
  1016.6 42.4 %reduce-scatter.25.cloned.1.call-start = ((), (), s32[]{:S(2)}) async-start(), calls=%async_computation.28 | async-start | bytes 491520 | tf_op jit(solution)/shard_map/reduce_scatter | solution.py:331
  1018.4 85.1 %all-reduce.60.cloned.1.call-start = ((), (), s32[]{:S(2)}) async-start(), calls=%async_computation.30 | async-start | bytes 786432 | tf_op jit(solution)/shard_map/psum | solution.py:79
  1019.2 86.5 %copy-start.137 = (bf16[256,3,64]{0,2,1:T(8,128)(2,1)}, bf16[256,3,64]{0,2,1:T(8,128)(2,1)S(1)}, u32[]{:S(2)}) copy-start(bf16[256,3,64]{0,2,1:T(8,128)(2,1)S(1)} %get-tuple-element.1294) | copy-start | bytes 294916
  1061.2 100.5 %all-reduce.62.cloned.1.call-start = ((), (), s32[]{:S(2)}) async-start(), calls=%async_computation.31 | async-start | bytes 786432 | tf_op jit(solution)/shard_map/psum | solution.py:79
  1108.2 3.6 collective-permute-start.5
  1113.5 50.4 %copy-start.51 = (bf16[256,768]{1,0:T(8,128)(2,1)}, bf16[256,768]{1,0:T(8,128)(2,1)S(1)}, u32[]{:S(2)}) copy-start(bf16[256,768]{1,0:T(8,128)(2,1)S(1)} %get-tuple-element.1171) | copy-start | bytes 1179652
  1117.5 98.9 %reduce-scatter.31.cloned.1.call-start = ((), (), s32[]{:S(2)}) async-start(), calls=%async_computation.33 | async-start | bytes 491520 | tf_op jit(solution)/shard_map/reduce_scatter | solution.py:334
  1195.7 42.2 %reduce-scatter.29.cloned.1.call-start = ((), (), s32[]{:S(2)}) async-start(), calls=%async_computation.32 | async-start | bytes 491520 | tf_op jit(solution)/shard_map/reduce_scatter | solution.py:331
  1197.7 84.9 %all-reduce.64.cloned.1.call-start = ((), (), s32[]{:S(2)}) async-start(), calls=%async_computation.34 | async-start | bytes 786432 | tf_op jit(solution)/shard_map/psum | solution.py:79
  1240.2 100.7 %all-reduce.66.cloned.1.call-start = ((), (), s32[]{:S(2)}) async-start(), calls=%async_computation.35 | async-start | bytes 786432 | tf_op jit(solution)/shard_map/psum | solution.py:79
  1287.2 4.0 collective-permute-start.6
  1292.0 51.2 %copy-start.53 = (bf16[256,768]{1,0:T(8,128)(2,1)}, bf16[256,768]{1,0:T(8,128)(2,1)S(1)}, u32[]{:S(2)}) copy-start(bf16[256,768]{1,0:T(8,128)(2,1)S(1)} %get-tuple-element.1173) | copy-start | bytes 1179652
  1296.0 100.7 %reduce-scatter.35.cloned.1.call-start = ((), (), s32[]{:S(2)}) async-start(), calls=%async_computation.37 | async-start | bytes 491520 | tf_op jit(solution)/shard_map/reduce_scatter | solution.py:334
  1376.0 42.4 %reduce-scatter.33.cloned.1.call-start = ((), (), s32[]{:S(2)}) async-start(), calls=%async_computation.36 | async-start | bytes 491520 | tf_op jit(solution)/shard_map/reduce_scatter | solution.py:331
  1382.4 80.5 %all-reduce.68.cloned.1.call-start = ((), (), s32[]{:S(2)}) async-start(), calls=%async_computation.38 | async-start | bytes 786432 | tf_op jit(solution)/shard_map/psum | solution.py:79
  1420.6 117.5 %all-reduce.70.cloned.1.call-start = ((), (), s32[]{:S(2)}) async-start(), calls=%async_computation.39 | async-start | bytes 786432 | tf_op jit(solution)/shard_map/psum | solution.py:79
  1467.6 20.5 %collective-permute-start.7 = (bf16[256,768]{1,0:T(8,128)(2,1)}, bf16[256,768]{1,0:T(8,128)(2,1)}, u32[]{:S(2)}, u32[]{:S(2)}) collective-permute-start(bf16[256,768]{1,0:T(8,128)(2,1)} %get-tuple-element.1186), channel_id=1, source_target_pairs={{16,0},{17,1},{18,2},{19,3},{20,4},{21,5},{22,6},{23,7},{24,8},{25... | collective-permute-start | bytes 1179656 | tf_op jit(solution)/shard_map/ppermute | solution.py:23
  1489.9 50.4 %copy-start.47 = (bf16[256,768]{1,0:T(8,128)(2,1)}, bf16[256,768]{1,0:T(8,128)(2,1)S(1)}, u32[]{:S(2)}) copy-start(bf16[256,768]{1,0:T(8,128)(2,1)S(1)} %get-tuple-element.1175) | copy-start | bytes 1179652
  1493.9 95.1 %reduce-scatter.39.cloned.1.call-start = ((), (), s32[]{:S(2)}) async-start(), calls=%async_computation.41 | async-start | bytes 491520 | tf_op jit(solution)/shard_map/reduce_scatter | solution.py:334
  1568.2 42.3 %reduce-scatter.37.cloned.1.call-start = ((), (), s32[]{:S(2)}) async-start(), calls=%async_computation.40 | async-start | bytes 491520 | tf_op jit(solution)/shard_map/reduce_scatter | solution.py:331
  1575.7 73.6 %reduce-scatter.45.cloned.1.call-start = ((), (), s32[]{:S(2)}) async-start(), calls=%async_computation.46 | async-start | bytes 491520
  1580.5 89.6 %all-reduce.72.cloned.1.call-start = ((), (), s32[]{:S(2)}) async-start(), calls=%async_computation.48 | async-start | bytes 1572864 | tf_op jit(solution)/shard_map/psum | solution.py:79
  1612.8 86.2 %reduce-scatter.47.cloned.1.call-start = ((), (), s32[]{:S(2)}) async-start(), calls=%async_computation.47 | async-start | bytes 1474560
  1619.7 81.5 %reduce-scatter.41.cloned.1.call-start = ((), (), s32[]{:S(2)}) async-start(), calls=%async_computation.42 | async-start | bytes 1474560 | tf_op jit(solution)/shard_map/reduce_scatter | solution.py:475
  1642.9 76.7 %reduce-scatter.43.cloned.1.call-start = ((), (), s32[]{:S(2)}) async-start(), calls=%async_computation.45 | async-start | bytes 1228800
  (302 other events, 3077.4 us)
Sparse Core Ops, SparseCore 0:
  131.7 42.5 all-reduce.35
  196.1 43.3 all-reduce.37
  282.5 43.9 all-reduce.39
  334.1 44.0 all-reduce.41
  420.9 43.9 all-reduce.43
  472.7 44.0 all-reduce.45
  560.9 44.3 all-reduce.47
  613.1 44.0 all-reduce.49
  700.5 44.4 all-reduce.51
  759.4 43.7 all-reduce.53
  881.9 42.1 all-reduce.55
  937.3 44.0 all-reduce.57
  1061.4 42.1 all-reduce.59
  1117.7 44.0 all-reduce.61
  1240.4 42.1 all-reduce.63
  1296.1 44.8 all-reduce.65
  1420.8 42.0 all-reduce.67
  1494.0 44.0 all-reduce.69
  1612.9 47.0 all-reduce.71
Sparse Core Ops, SparseCore 1:
  133.7 28.6 all-gather.29
  164.0 29.4 all-gather.27
  837.1 20.6 reduce-scatter.22
  860.8 18.7 reduce-scatter.20
  1016.7 20.5 reduce-scatter.26
  1040.2 18.7 reduce-scatter.24
  1195.8 20.5 reduce-scatter.30
  1219.2 18.7 reduce-scatter.28
  1376.1 20.5 reduce-scatter.34
  1399.6 18.7 reduce-scatter.32
  1568.3 20.6 reduce-scatter.38
  1591.9 18.6 reduce-scatter.36
  1613.4 18.8 reduce-scatter.44
  1634.6 27.1 reduce-scatter.46
  1664.1 28.3 reduce-scatter.40
  1694.8 24.7 reduce-scatter.42
where the time goes:
time: 1740 us; the launch traced here: 1730 us
  waiting for transfers between devices  818 us (47%)
  blocking collectives  396 us (23%)
  matrix products  171 us (10%)
  other arithmetic  150 us (9%)
  local copies, waits for them, and re-layouts  141 us (8%)
  between operations  21 us (1%)
  loops' own time  19.5 us (1%)
    psum x9, waiting for transfers between devices, branch_sum(): lax.psum(partial_value.astype(jnp.bfloat16), 'tensor').astype(jnp.float32)  338 us
    psum x10, waiting for transfers between devices, grad_sum(): lax.psum(partial_value.astype(jnp.bfloat16), 'tensor').astype(jnp.float32)  265 us
    all_gather x10, blocking collectives, taken_in(): lax.all_gather(a, axis, axis=dim, tiled=True)  150 us
    reduce_scatter x5, waiting for transfers between devices, layer_backward(): lax.psum_scatter(grad_keys.astype(jnp.bfloat16), 'ctx', scatter_dimension...  108 us
    all_gather x5, blocking collectives, layer_backward(): lax.all_gather(value_rows, 'ctx', axis=0, tiled=True)  76.2 us
    all_gather x5, blocking collectives, layer_backward(): lax.all_gather(key_rows, 'ctx', axis=0, tiled=True)  74.9 us
    reduce_scatter x5, waiting for transfers between devices, layer_backward(): lax.psum_scatter(grad_values.astype(jnp.bfloat16), 'ctx', scatter_dimensi...  69.3 us
    unnamed x593, local copies, waits for them, and re-layouts  46 us
  transfers between devices with their start and end apart: 43, of which 33 were waited for; matrix products, arithmetic and copies ran while one was open for 9% of the time, Pallas kernels for 0%

commit v1 on v0

v1 whole, which is shorter than its diff:
```python
import math

import jax
import jax.numpy as jnp
from jax import lax
from jax.sharding import PartitionSpec as P

HEAD = 64
NORM_EPS = 1e-05
NEG_BIG = -1e30
BF = jnp.bfloat16
F32 = jnp.float32
ROWS = ("tensor", "ctx")


def norm_parts(x, gain, shift):
    mean = jnp.mean(x, axis=-1, keepdims=True)
    centered = x - mean
    inverse = lax.rsqrt(jnp.mean(centered * centered, axis=-1, keepdims=True) + NORM_EPS)
    normal = centered * inverse
    return normal * gain + shift, normal, inverse


def norm_back(upstream, normal, inverse, gain):
    scaled = upstream * gain
    return inverse * (
        scaled
        - jnp.mean(scaled, axis=-1, keepdims=True)
        - normal * jnp.mean(scaled * normal, axis=-1, keepdims=True)
    )


def act(u):
    return jax.nn.gelu(u, approximate=True)


def dot(spec, a, b):
    return jnp.einsum(spec, a, b, preferred_element_type=F32)


def heads(a):
    return a.reshape(a.shape[0], a.shape[1], a.shape[2] // HEAD, HEAD)


def attend(q, k, v, allowed):
    scores = jnp.where(allowed, dot("tnhd,tmhd->thnm", heads(q), heads(k)), NEG_BIG)
    top = jnp.max(scores, axis=-1, keepdims=True)
    total = jnp.sum(jnp.where(allowed, jnp.exp(scores - top), 0.0), axis=-1, keepdims=True)
    lse = top + jnp.log(total)
    chances = jnp.where(allowed, jnp.exp(scores - lse), 0.0).astype(BF)
    out = dot("thnm,tmhd->tnhd", chances, heads(v))
    return out.reshape(q.shape).astype(BF), lse


def attend_back(q, k, v, lse, allowed, d_out):
    scores = dot("tnhd,tmhd->thnm", heads(q), heads(k))
    chances = jnp.where(allowed, jnp.exp(scores - lse), 0.0)
    d_chance = dot("tnhd,tmhd->thnm", heads(d_out), heads(v))
    delta = jnp.sum(chances * d_chance, axis=-1, keepdims=True)
    d_score = (chances * (d_chance - delta)).astype(BF)
    d_v = dot("thnm,tnhd->tmhd", chances.astype(BF), heads(d_out))
    d_k = dot("thnm,tnhd->tmhd", d_score, heads(q))
    d_q = dot("thnm,tmhd->tnhd", d_score, heads(k))
    return d_q.reshape(q.shape), d_k.reshape(k.shape), d_v.reshape(v.shape)


def forward(x_ctx, weights, vecs, allowed):
    w_attn, w_mlp = weights
    part = w_attn.shape[2] // 4
    hidden = w_mlp.shape[2] // 2
    bias_q, bias_v, bias_up, ln1_g, ln1_b, bias_out, ln2_g, ln2_b, bias_down = vecs
    rows = allowed.shape[0]
    h_ctx, normal_ctx, inverse_ctx = norm_parts(x_ctx.astype(F32), ln1_g, ln1_b)
    h_ctx = h_ctx.astype(BF)
    x = x_ctx[-rows:].astype(F32)
    q = (dot("nd,tdk->tnk", h_ctx[-rows:], w_attn[:, :, :part]) + bias_q) / math.sqrt(HEAD)
    q = q.astype(BF)
    k = dot("nd,tdk->tnk", h_ctx, w_attn[:, :, part : 2 * part]).astype(BF)
    v = (dot("nd,tdk->tnk", h_ctx, w_attn[:, :, 2 * part : 3 * part]) + bias_v).astype(BF)
    o, lse = attend(q, k, v, allowed)
    middle = x + dot("tnk,tdk->nd", o, w_attn[:, :, 3 * part :]) + bias_out
    h2, normal2, inverse2 = norm_parts(middle, ln2_g, ln2_b)
    h2 = h2.astype(BF)
    raised = dot("nd,tdf->tnf", h2, w_mlp[:, :, :hidden]) + bias_up
    active = act(raised).astype(BF)
    y = middle + dot("tnf,tdf->nd", active, w_mlp[:, :, hidden:]) + bias_down
    saved = (
        h_ctx,
        normal_ctx[-rows:],
        inverse_ctx[-rows:],
        q,
        k,
        v,
        o,
        lse,
        h2,
        normal2,
        inverse2,
        raised,
        active,
    )
    return y, saved


def send_back(d_ctx, rows, window):
    total = d_ctx[-rows:]
    count = lax.axis_size("ctx")
    low = d_ctx[:-rows].astype(BF)
    for step in range(1, window + 1):
        start = (window - step) * rows
        total = total + lax.ppermute(
            low[start : start + rows], "ctx", [(i, i - step) for i in range(step, count)]
        ).astype(F32)
    return total


def backward(upstream, saved, weights, vecs, allowed, window, want_grads):
    w_attn, w_mlp = weights
    part = w_attn.shape[2] // 4
    hidden = w_mlp.shape[2] // 2
    ln1_g, ln2_g = vecs[3], vecs[6]
    h_ctx, normal1, inverse1, q, k, v, o, lse, h2, normal2, inverse2, raised, active = saved
    rows = allowed.shape[0]
    up_low = upstream.astype(BF)
    d_active = dot("nd,tdf->tnf", up_low, w_mlp[:, :, hidden:])
    d_raised = jax.vjp(act, raised)[1](d_active)[0].astype(BF)
    d_h2 = dot("tnf,tdf->nd", d_raised, w_mlp[:, :, :hidden])
    d_mid = upstream + norm_back(d_h2, normal2, inverse2, ln2_g)
    d_branch = d_mid.astype(BF)
    d_out = dot("nd,tdk->tnk", d_branch, w_attn[:, :, 3 * part :]).astype(BF)
    d_q, d_k, d_v = attend_back(q, k, v, lse, allowed, d_out)
    d_q = d_q.astype(BF) / math.sqrt(HEAD)
    d_k = d_k.astype(BF)
    d_v = d_v.astype(BF)
    d_ctx = dot("tnk,tdk->nd", d_k, w_attn[:, :, part : 2 * part]) + dot(
        "tnk,tdk->nd", d_v, w_attn[:, :, 2 * part : 3 * part]
    )
    d_own = dot("tnk,tdk->nd", d_q, w_attn[:, :, :part])
    d_h = send_back(d_ctx, rows, window) + d_own
    d_x = d_mid + norm_back(d_h, normal1, inverse1, ln1_g)
    if not want_grads:
        return d_x
    mlp_grad = jnp.concatenate(
        [
            dot("nd,tnf->tdf", h2, d_raised).astype(BF),
            dot("nd,tnf->tdf", up_low, active).astype(BF),
        ],
        axis=2,
    )
    attn_grad = jnp.concatenate(
        [
            dot("nd,tnk->tdk", h_ctx[-rows:], d_q).astype(BF),
            dot("nd,tnk->tdk", h_ctx, d_k).astype(BF),
            dot("nd,tnk->tdk", h_ctx, d_v).astype(BF),
            dot("nd,tnk->tdk", d_branch, o).astype(BF),
        ],
        axis=2,
    )
    flat = [
        jnp.sum(d_h * normal1, axis=0),
        jnp.sum(d_h, axis=0),
        jnp.sum(d_branch.astype(F32), axis=0),
        jnp.sum(d_h2 * normal2, axis=0),
        jnp.sum(d_h2, axis=0),
        jnp.sum(up_low.astype(F32), axis=0),
        jnp.sum(d_q.astype(F32), axis=1).reshape(-1),
        jnp.sum(d_v.astype(F32), axis=1).reshape(-1),
        jnp.sum(d_raised.astype(F32), axis=1).reshape(-1),
    ]
    return d_x, mlp_grad, attn_grad, jnp.concatenate(flat)


def local(
    boundary_in,
    segments,
    ln1_gain,
    ln1_bias,
    w_qkv,
    b_qv,
    w_out,
    b_out,
    ln2_gain,
    ln2_bias,
    w_up,
    b_up,
    w_down,
    b_down,
):
    section = lax.axis_index("section")
    ctx = lax.axis_index("ctx")
    tensor = lax.axis_index("tensor")
    n_ctx = lax.axis_size("ctx")
    n_tensor = lax.axis_size("tensor")
    rows = boundary_in.shape[2]
    seq = segments.shape[1]
    own_d, part = w_out.shape[2], w_out.shape[1]
    hidden = w_up.shape[2]
    width = own_d * n_ctx
    window = min(n_ctx - 1, (seq // 2 - 1 + rows - 1) // rows)

    x_own = lax.dynamic_index_in_dim(boundary_in[0], tensor, 0, keepdims=False)
    x_blocks = [
        lax.ppermute(x_own, "ctx", [(i, i + step) for i in range(n_ctx - step)])
        for step in range(window, 0, -1)
    ] + [x_own]

    vec_own = jnp.concatenate(
        [
            b_up[0],
            b_qv[0].reshape(-1),
            ln1_gain[0],
            ln1_bias[0],
            b_out[0],
            ln2_gain[0],
            ln2_bias[0],
            b_down[0],
        ]
    )
    vec_all = lax.all_gather(vec_own[None], ROWS, axis=0, tiled=True).astype(F32)
    vec_all = vec_all.reshape(n_tensor, n_ctx, -1)
    attn_own = jnp.concatenate(
        [jnp.transpose(w_qkv[0], (1, 0, 2)).reshape(own_d, 3 * part), jnp.transpose(w_out[0])], axis=1
    )
    mlp_own = jnp.concatenate([w_up[0], jnp.transpose(w_down[0])], axis=1)
    w_attn = lax.all_gather(attn_own, ROWS, axis=0, tiled=True).reshape(n_tensor, width, -1)
    w_mlp = lax.all_gather(mlp_own, ROWS, axis=0, tiled=True).reshape(n_tensor, width, -1)
    weights = (w_attn, w_mlp)
    per_tensor = vec_all[:, 0, :, None]
    bias_up = per_tensor[:, :hidden].reshape(n_tensor, 1, hidden)
    bias_q = per_tensor[:, hidden : hidden + part].reshape(n_tensor, 1, part)
    bias_v = per_tensor[:, hidden + part : hidden + 2 * part].reshape(n_tensor, 1, part)
    wide = vec_all[0, :, hidden + 2 * part :].reshape(n_ctx, 6, own_d)
    wide = jnp.transpose(wide, (1, 0, 2)).reshape(6, width)
    vecs = (bias_q, bias_v, bias_up) + tuple(wide[i] for i in range(6))

    seg = lax.dynamic_index_in_dim(segments, tensor, 0, keepdims=False)
    seg_pad = jnp.concatenate([jnp.full((window * rows,), -1, jnp.int32), seg])
    seg_keys = lax.dynamic_slice_in_dim(seg_pad, ctx * rows, (window + 1) * rows)
    seg_rows = seg_keys[-rows:]
    key_pos = jnp.arange((window + 1) * rows, dtype=jnp.int32) - window * rows
    row_pos = jnp.arange(rows, dtype=jnp.int32)
    allowed = (seg_rows[:, None] == seg_keys[None, :]) & (key_pos[None, :] <= row_pos[:, None])

    first, unused = forward(jnp.concatenate(x_blocks), weights, vecs, allowed)
    first_low = first.astype(BF)
    passed = [
        lax.ppermute(
            first_low,
            ("section", "ctx"),
            [(i, n_ctx + i + step) for i in range(n_ctx - step)],
        )
        for step in range(window, -1, -1)
    ]
    chosen = [jnp.where(section == 0, a, b) for a, b in zip(x_blocks, passed)]
    result, saved = forward(jnp.concatenate(chosen), weights, vecs, allowed)

    upper = backward(x_own.astype(F32), saved, weights, vecs, allowed, window, False)
    returned = lax.ppermute(upper.astype(BF), "section", [(1, 0)])
    upstream = jnp.where(section == 0, returned, x_own).astype(F32)
    d_x, mlp_grad, attn_grad, flat = backward(
        upstream, saved, weights, vecs, allowed, window, True
    )

    mlp_sum = lax.psum_scatter(
        mlp_grad.reshape(n_tensor * width, -1), ROWS, scatter_dimension=0, tiled=True
    ).astype(F32)
    attn_sum = lax.psum_scatter(
        attn_grad.reshape(n_tensor * width, -1), ROWS, scatter_dimension=0, tiled=True
    ).astype(F32)
    flat = lax.psum(flat, ROWS)
    ends = lax.all_gather(
        jnp.where(section == 0, d_x, result).astype(BF), "tensor", axis=0
    ).astype(F32)

    wide_sum = lax.dynamic_slice_in_dim(flat[: 6 * width].reshape(6, width), ctx * own_d, own_d, 1)
    qv_sum = flat[6 * width : 6 * width + 2 * n_tensor * part].reshape(2, n_tensor, part)
    qv_sum = lax.dynamic_index_in_dim(qv_sum, tensor, 1, keepdims=False)
    up_sum = flat[6 * width + 2 * n_tensor * part :].reshape(n_tensor, hidden)
    up_sum = lax.dynamic_index_in_dim(up_sum, tensor, 0, keepdims=False)
    g_qkv = jnp.transpose(attn_sum[:, : 3 * part].reshape(own_d, 3, part), (1, 0, 2))
    g_out = jnp.transpose(attn_sum[:, 3 * part :])
    g_up = mlp_sum[:, :hidden]
    g_down = jnp.transpose(mlp_sum[:, hidden:])
    return (
        ends[None],
        wide_sum[0][None],
        wide_sum[1][None],
        g_qkv[None],
        qv_sum[None],
        g_out[None],
        wide_sum[2][None],
        wide_sum[3][None],
        wide_sum[4][None],
        g_up[None],
        up_sum[None],
        g_down[None],
        wide_sum[5][None],
    )


def solution(mesh):
    in_specs = (
        P("section", None, "ctx", None),
        P(),
        P("section", "ctx"),
        P("section", "ctx"),
        P("section", None, "ctx", "tensor"),
        P("section", None, "tensor"),
        P("section", "tensor", "ctx"),
        P("section", "ctx"),
        P("section", "ctx"),
        P("section", "ctx"),
        P("section", "ctx", "tensor"),
        P("section", "tensor"),
        P("section", "tensor", "ctx"),
        P("section", "ctx"),
    )
    out_specs = (
        P("section", None, "ctx", None),
        P("section", "ctx"),
        P("section", "ctx"),
        P("section", None, "ctx", "tensor"),
        P("section", None, "tensor"),
        P("section", "tensor", "ctx"),
        P("section", "ctx"),
        P("section", "ctx"),
        P("section", "ctx"),
        P("section", "ctx", "tensor"),
        P("section", "tensor"),
        P("section", "tensor", "ctx"),
        P("section", "ctx"),
    )
    return jax.shard_map(local, mesh=mesh, in_specs=in_specs, out_specs=out_specs, check_vma=False)
```

time: 1740 us -> 768 us (0.44)
  waiting for transfers between devices: 818 us -> 408 us
  blocking collectives: 396 us -> 139 us
  other arithmetic: 150 us -> 32 us
  local copies, waits for them, and re-layouts: 141 us -> 33.4 us
  matrix products: 171 us -> 111 us
  loops' own time: 19.5 us -> 0 us
    psum x19 -> x0, waiting for transfers between devices: 602 us -> none  [the longest x9 338 us: branch_sum(): lax.psum(partial_value.astype(jnp.bfloat16), 'tensor').astype(jnp.float32)]
    all_gather x22 -> x1, blocking collectives: 349 us -> 58 us  [local(): lax.all_gather(vec_own[None], ROWS, axis=0, tiled=True).astype(F32)]
    all_gather x2 -> x3, waiting for transfers between devices: 12.9 us -> 127 us  [the longest x1 107 us: local(): lax.all_gather(mlp_own, ROWS, axis=0, tiled=True)]
    psum x1, blocking collectives: 9.07 us -> 81.3 us  [local(): flat = lax.psum(flat, ROWS)]
    reduce_sum x59 -> x10, other arithmetic: 68.2 us -> 7.92 us  [the longest x2 5.58 us: attend(): jnp.sum(jnp.where(allowed, jnp.exp(scores - top), 0.0), axis=-1, keepdims...]
    dot_general x115 -> x40, matrix products: 167 us -> 111 us  [dot(): return jnp.einsum(spec, a, b, preferred_element_type=F32)]
    reduce_scatter x11 -> x2, waiting for transfers between devices: 178 us -> 230 us  [the longest x1 173 us: local(): lax.psum_scatter(mlp_grad.reshape(n_tensor * width, -1), ROWS, scatter_di...]
    dynamic_slice x46 -> x3, local copies, waits for them, and re-layouts: 45.2 us -> 0.6 us  [the longest x1 0.59 us: local(): up_sum = lax.dynamic_index_in_dim(up_sum, tensor, 0, keepdims=False)]
  transfers between devices with their start and end apart: 43 -> 15, of which waited for: 33 -> 9; matrix products, arithmetic and copies ran while one was open for 9% -> 9% of each run, Pallas kernels for 0% -> 0%
where the time goes in v1:
time: 768 us; the launch traced here: 762 us
  waiting for transfers between devices  408 us (53%)
  blocking collectives  139 us (18%)
  matrix products  111 us (14%)
  local copies, waits for them, and re-layouts  33.4 us (4%)
  other arithmetic  32 us (4%)
  starting transfers between devices  22.8 us (3%)
  between operations  15.8 us (2%)
    reduce_scatter x1, waiting for transfers between devices, local(): lax.psum_scatter(mlp_grad.reshape(n_tensor * width, -1), ROWS, scatter_di...  173 us
    dot_general x40, matrix products, dot(): return jnp.einsum(spec, a, b, preferred_element_type=F32)  111 us
    all_gather x1, waiting for transfers between devices, local(): lax.all_gather(mlp_own, ROWS, axis=0, tiled=True)  107 us
    psum x1, blocking collectives, local(): flat = lax.psum(flat, ROWS)  81.3 us
    all_gather x1, blocking collectives, local(): lax.all_gather(vec_own[None], ROWS, axis=0, tiled=True).astype(F32)  58 us
    reduce_scatter x1, waiting for transfers between devices, local(): lax.psum_scatter(attn_grad.reshape(n_tensor * width, -1), ROWS, scatter_d...  56.2 us
    ppermute x4, waiting for transfers between devices, send_back(): lax.ppermute(low[start:start + rows], 'ctx', [(i, i - step) for i in rang...  41.1 us
    all_gather x1, waiting for transfers between devices, local(): lax.all_gather(attn_own, ROWS, axis=0, tiled=True)  20.5 us
  transfers between devices with their start and end apart: 15, of which 9 were waited for; matrix products, arithmetic and copies ran while one was open for 9% of the time, Pallas kernels for 0%

profile of v1, /device:TPU:0, one launch (start us, length us, event | category | flops | bytes accessed | tf_op | source)
XLA Modules:
  0.0 762.0 jit_solution(5446049037634792109)
XLA Ops:
  7.3 1.2 copy.90
  10.5 1.9 pad_maximum_fusion.4
  12.5 5.0 collective-permute-start.1
  17.5 4.5 collective-permute-start
  22.4 58.0 %all-gather.2 = bf16[16,1,2304]{2,1,0:T(2,128)(2,1)S(1)} all-gather(bf16[1,1,2304]{2,1,0:T(2,128)(2,1)S(1)} %reshape.321), channel_id=2, replica_groups=mesh['section'=2,'ctx'=4,'tensor'=4] {'tensor','ctx'}, dimensions={0}, use_global_device_ids=true | all-gather | bytes 78336 | tf_op jit(solution)/shard_map/all_gather | solution.py:219
  82.6 1.5 fusion.51
  84.2 20.5 %all-gather.7.cloned.1.call-done = bf16[3072,768]{1,0:T(8,128)(2,1)} async-done(((bf16[192,768]{1,0:T(8,128)(2,1)}), bf16[3072,768]{1,0:T(8,128)(2,1)}) %all-gather.7.cloned.1.call-update) | async-done | bytes 4718608 | tf_op jit(solution)/shard_map/all_gather | solution.py:225
  104.7 2.2 fusion.145
  106.9 3.7 convolution_convert_fusion.7
  110.6 1.7 select_reduce_fusion.3
  112.3 2.9 select_reduce_fusion.1
  115.2 1.6 add_convert_fusion.2
  116.9 3.0 fusion.144
  122.3 106.9 %all-gather.9.cloned.1.call-done = bf16[3072,1536]{1,0:T(8,128)(2,1)} async-done(((bf16[192,1536]{1,0:T(8,128)(2,1)}), bf16[3072,1536]{1,0:T(8,128)(2,1)}) %all-gather.9.cloned.1.call-update) | async-done | bytes 9437200 | tf_op jit(solution)/shard_map/all_gather | solution.py:226
  229.2 9.9 %fusion.136 = bf16[256,768]{1,0:T(8,128)(2,1)} fusion(f32[256,768]{1,0:T(8,128)} %copy-done.21, bf16[4,768,1536]{2,1,0:T(8,128)(2,1)} %bitcast.371, f32[4,768]{1,0:T(4,128)S(1)} %bitcast.365, f32[768]{0:T(1024)S(1)} %add.298, f32[768]{0:T(1024)S(1)} %add.288, f32[768]{0:T(1024)S(1)} %mul.288, f32[256]{0:T(256)S(1)} %add_rsqrt_fusion.3, ...), kind=kOutput, calls=%fused_computation.137 | convolution fusion | flops 2425356288 | bytes 11426816 | tf_op jit(solution)/shard_map/tnf,tdf->nd/dot_general | solution.py:38
  239.0 2.0 collective-permute-start.2
  241.1 2.0 collective-permute-start.4
  243.1 1.5 collective-permute-start.3
  244.7 3.2 collective-permute-done.4
  248.0 4.2 collective-permute-done.3
  253.0 2.0 fusion.45
  255.0 3.5 add_convert_fusion
  259.1 2.0 convolution_convert_fusion.6
  261.1 1.6 select_reduce_fusion.2
  262.7 2.7 select_reduce_fusion
  266.4 3.4 fusion.143
  272.2 3.1 fusion.37
  275.3 11.3 %fusion.229 = (f32[256]{0:T(256)S(1)}, f32[256]{0:T(256)S(1)}, f32[256,768]{1,0:T(8,128)}) fusion(f32[256,768]{1,0:T(8,128)S(1)} %subtract_multiply_fusion.1, f32[768]{0:T(1024)S(1)} %mul.288, bf16[4,768,1536]{2,1,0:T(8,128)(2,1)} %bitcast.372, f32[4,768,256]{2,1,0:T(8,128)} %fusion.37, f32[4,768]{1,0:T(4,128)S(1)} %bitcast.366, ...), kind=kOutput, calls=%fused_computation.296 | convolution fusion | flops 2433220096 | bytes 14566404 | tf_op jit(solution)/shard_map/tnf,tdf->nd/dot_general | solution.py:38
  286.6 2.9 convolution_convert_fusion.11
  289.6 5.5 fusion.79
  295.1 6.1 multiply_reduce_fusion.1
  301.2 2.5 multiply_convert_fusion.1
  304.7 4.0 fusion.159
  308.7 1.5 fusion.241
  310.3 1.3 collective-permute-start.6
  311.6 1.4 collective-permute-start.5
  313.0 1.5 fusion.147
  314.6 18.9 %collective-permute-done.6 = bf16[256,768]{1,0:T(8,128)(2,1)S(1)} collective-permute-done((bf16[256,768]{1,0:T(8,128)(2,1)S(1)}, bf16[256,768]{1,0:T(8,128)(2,1)S(1)}, u32[]{:S(2)}, u32[]{:S(2)}) %collective-permute-start.6) | collective-permute-done | bytes 393248 | tf_op jit(solution)/shard_map/ppermute | solution.py:111
  334.8 1.6 collective-permute-start.7
  336.4 2.3 collective-permute-done.7
  338.9 6.2 convert_reduce_fusion
  345.1 1.6 multiply_reduce_fusion.2
  347.1 2.8 convolution_convert_fusion.9
  349.9 2.4 convert_reduce_fusion.3
  352.4 3.4 multiply_reduce_fusion
  355.7 2.7 multiply_convert_fusion
  359.4 4.4 fusion.163
  363.9 1.5 fusion.242
  365.5 1.6 collective-permute-start.9
  367.0 1.4 collective-permute-start.8
  368.5 1.6 convert_reduce_fusion.5
  370.1 22.1 %collective-permute-done.9 = bf16[256,768]{1,0:T(8,128)(2,1)S(1)} collective-permute-done((bf16[256,768]{1,0:T(8,128)(2,1)S(1)}, bf16[256,768]{1,0:T(8,128)(2,1)S(1)}, u32[]{:S(2)}, u32[]{:S(2)}) %collective-permute-start.9) | collective-permute-done | bytes 393248 | tf_op jit(solution)/shard_map/ppermute | solution.py:111
  393.3 3.5 select_convert_fusion.8
  397.4 1.6 fusion.88
  401.4 2.3 pad_maximum_fusion.1
  403.7 6.7 copy.109
  411.8 1.4 convert_bitcast_fusion.1
  413.7 2.4 convert_bitcast_fusion
  416.1 4.0 pad_maximum_fusion
  420.1 12.7 %copy.111 = bf16[4,768,1536]{2,1,0:T(8,128)(2,1)} copy(bf16[4,768,1536]{1,2,0:T(8,128)(2,1)} %pad_maximum_fusion) | data formatting | bytes 18874368 | tf_op jit(solution)/shard_map/concatenate | solution.py:143
  433.1 81.3 %psum.7 = f32[9216]{0:T(1024)S(1)} all-reduce(f32[9216]{0:T(1024)S(1)} %constant_dynamic-update-slice_fusion), channel_id=1, replica_groups=mesh['section'=2,'ctx'=4,'tensor'=4] {'tensor','ctx'}, use_global_device_ids=true, to_apply=%region_31.32 | all-reduce | flops 9216 | bytes 73728 | tf_op jit(solution)/shard_map/psum | solution.py:270
  516.4 3.3 convert.10
  519.8 56.2 %reduce-scatter.3.cloned.1.call-done = bf16[192,768]{1,0:T(8,128)(2,1)} async-done(((bf16[3072,768]{1,0:T(8,128)(2,1)}), bf16[192,768]{1,0:T(8,128)(2,1)}) %reduce-scatter.3.cloned.1.call-update) | async-done | bytes 294928 | tf_op jit(solution)/shard_map/reduce_scatter | solution.py:267
  579.2 173.4 %reduce-scatter.5.cloned.1.call-done = bf16[192,1536]{1,0:T(8,128)(2,1)} async-done(((bf16[3072,1536]{1,0:T(8,128)(2,1)}), bf16[192,1536]{1,0:T(8,128)(2,1)}) %reduce-scatter.5.cloned.1.call-update) | async-done | bytes 589840 | tf_op jit(solution)/shard_map/reduce_scatter | solution.py:264
  (248 shorter events, 28.9 us)
Async XLA Ops:
  7.2 74.0 %copy-start = (s32[4,1024]{1,0:T(4,128)S(1)}, s32[4,1024]{1,0:T(4,128)}, u32[]{:S(2)}) copy-start(s32[4,1024]{1,0:T(4,128)} %param.15) | copy-start | bytes 49156
  7.2 5.3 copy-start.12
  7.2 14.8 %copy-start.26 = (bf16[1,2,192]{2,1,0:T(2,128)(2,1)S(1)}, bf16[1,2,192]{2,1,0:T(2,128)(2,1)}, u32[]{:S(2)}) copy-start(bf16[1,2,192]{2,1,0:T(2,128)(2,1)} %param.19) | copy-start | bytes 2308
  7.2 14.8 %copy-start.25 = (bf16[1,768]{1,0:T(2,128)(2,1)S(1)}, bf16[1,768]{1,0:T(2,128)(2,1)}, u32[]{:S(2)}) copy-start(bf16[1,768]{1,0:T(2,128)(2,1)} %param.25) | copy-start | bytes 4612
  7.2 14.9 %copy-start.27 = (bf16[1,192]{1,0:T(2,128)(2,1)S(1)}, bf16[1,192]{1,0:T(2,128)(2,1)}, u32[]{:S(2)}) copy-start(bf16[1,192]{1,0:T(2,128)(2,1)} %param.16) | copy-start | bytes 1156
  7.2 14.9 %copy-start.28 = (bf16[1,192]{1,0:T(2,128)(2,1)S(1)}, bf16[1,192]{1,0:T(2,128)(2,1)}, u32[]{:S(2)}) copy-start(bf16[1,192]{1,0:T(2,128)(2,1)} %param.17) | copy-start | bytes 1156
  7.3 14.9 %copy-start.29 = (bf16[1,192]{1,0:T(2,128)(2,1)S(1)}, bf16[1,192]{1,0:T(2,128)(2,1)}, u32[]{:S(2)}) copy-start(bf16[1,192]{1,0:T(2,128)(2,1)} %param.21) | copy-start | bytes 1156
  7.3 14.9 %copy-start.30 = (bf16[1,192]{1,0:T(2,128)(2,1)S(1)}, bf16[1,192]{1,0:T(2,128)(2,1)}, u32[]{:S(2)}) copy-start(bf16[1,192]{1,0:T(2,128)(2,1)} %param.22) | copy-start | bytes 1156
  7.3 14.9 %copy-start.31 = (bf16[1,192]{1,0:T(2,128)(2,1)S(1)}, bf16[1,192]{1,0:T(2,128)(2,1)}, u32[]{:S(2)}) copy-start(bf16[1,192]{1,0:T(2,128)(2,1)} %param.23) | copy-start | bytes 1156
  7.3 15.0 %copy-start.32 = (bf16[1,192]{1,0:T(2,128)(2,1)S(1)}, bf16[1,192]{1,0:T(2,128)(2,1)}, u32[]{:S(2)}) copy-start(bf16[1,192]{1,0:T(2,128)(2,1)} %param.27) | copy-start | bytes 1156
  7.3 97.4 %all-gather.7.cloned.1.call-start = ((), (), s32[]{:S(2)}) async-start(), calls=%async_computation.2 | async-start | bytes 5013504 | tf_op jit(solution)/shard_map/all_gather | solution.py:225
  10.4 218.8 %all-gather.9.cloned.1.call-start = ((), (), s32[]{:S(2)}) async-start(), calls=%async_computation.3 | async-start | bytes 10027008 | tf_op jit(solution)/shard_map/all_gather | solution.py:226
  12.4 504.0 %all-gather.11.cloned.1.call-start = ((), (), s32[]{:S(2)}) async-start(), calls=%async_computation.6 | async-start | bytes 1966080 | tf_op jit(solution)/shard_map/all_gather | solution.py:271
  12.5 69.4 %collective-permute-start.1 = (bf16[256,768]{1,0:T(8,128)(2,1)S(1)}, bf16[256,768]{1,0:T(8,128)(2,1)S(1)}, u32[]{:S(2)}, u32[]{:S(2)}) collective-permute-start(bf16[256,768]{1,0:T(8,128)(2,1)S(1)} %dynamic-slice_bitcast_fusion), channel_id=1, source_target_pairs={{0,4},{4,8},{8,12},{1,5},{5,9},{9,13},{2,6},{6,10},{10,14},{3,7},{... | collective-permute-start | bytes 1179656 | tf_op jit(solution)/shard_map/ppermute | solution.py:203
  17.5 64.4 %collective-permute-start = (bf16[256,768]{1,0:T(8,128)(2,1)S(1)}, bf16[256,768]{1,0:T(8,128)(2,1)S(1)}, u32[]{:S(2)}, u32[]{:S(2)}) collective-permute-start(bf16[256,768]{1,0:T(8,128)(2,1)S(1)} %dynamic-slice_bitcast_fusion), channel_id=1, source_target_pairs={{0,8},{4,12},{1,9},{5,13},{2,10},{6,14},{3,11},{7,15},{16,24},{20,... | collective-permute-start | bytes 1179656 | tf_op jit(solution)/shard_map/ppermute | solution.py:203
  106.9 8.3 %slice-start.12 = ((s8[4718592]{0:T(1024)(128)(4,1)}), s8[4194304]{0:T(1024)(128)(4,1)S(1)}, s32[]{:S(2)}) async-start(s8[4718592]{0:T(1024)(128)(4,1)} %bitcast.390), calls=%async_computation.19 | async-start | bytes 8388608
  110.6 4.6 slice-start.13
  239.0 5.6 collective-permute-start.2
  241.1 6.9 collective-permute-start.4
  243.1 9.1 %collective-permute-start.3 = (bf16[256,768]{1,0:T(8,128)(2,1)}, bf16[256,768]{1,0:T(8,128)(2,1)S(1)}, u32[]{:S(2)}, u32[]{:S(2)}) collective-permute-start(bf16[256,768]{1,0:T(8,128)(2,1)} %fusion.136), channel_id=1, source_target_pairs={{0,24},{4,28},{1,25},{5,29},{2,26},{6,30},{3,27},{7,31}} | collective-permute-start | bytes 1179656 | tf_op jit(solution)/shard_map/ppermute | solution.py:247
  252.3 6.2 slice-start.14
  253.0 5.5 slice-start.15
  255.0 4.1 copy-start.10
  258.5 7.0 copy-start.3
  262.7 3.7 copy-start.2
  265.5 6.6 slice-start.3
  266.4 5.7 slice-start.4
  266.4 5.8 slice-start.5
  289.5 5.6 copy-start.4
  289.5 11.7 %slice-start = ((s8[9437184]{0:T(1024)(128)(4,1)}), s8[4194304]{0:T(1024)(128)(4,1)S(1)}, s32[]{:S(2)}) async-start(s8[9437184]{0:T(1024)(128)(4,1)} %bitcast.328), calls=%async_computation.7 | async-start | bytes 8388608
  289.5 11.7 %slice-start.1 = ((s8[9437184]{0:T(1024)(128)(4,1)}), s8[4194304]{0:T(1024)(128)(4,1)S(1)}, s32[]{:S(2)}) async-start(s8[9437184]{0:T(1024)(128)(4,1)} %bitcast.328), calls=%async_computation.8 | async-start | bytes 8388608
  295.1 6.1 slice-start.2
  303.7 5.0 slice-start.16
  304.7 4.0 slice-start.17
  310.3 23.2 %collective-permute-start.6 = (bf16[256,768]{1,0:T(8,128)(2,1)S(1)}, bf16[256,768]{1,0:T(8,128)(2,1)S(1)}, u32[]{:S(2)}, u32[]{:S(2)}) collective-permute-start(bf16[256,768]{1,0:T(8,128)(2,1)S(1)} %get-tuple-element.83), channel_id=1, source_target_pairs={{8,0},{12,4},{9,1},{13,5},{10,2},{14,6},{11,3},{15,7},{24,16},{28,... | collective-permute-start | bytes 1179656 | tf_op jit(solution)/shard_map/ppermute | solution.py:111
  311.6 21.9 %copy-start.5 = (f32[768,768]{1,0:T(8,128)S(1)}, f32[768,768]{1,0:T(8,128)}, u32[]{:S(2)}) copy-start(f32[768,768]{1,0:T(8,128)} %get-tuple-element.76) | copy-start | bytes 7077892
  311.6 21.9 %collective-permute-start.5 = (bf16[256,768]{1,0:T(8,128)(2,1)S(1)}, bf16[256,768]{1,0:T(8,128)(2,1)S(1)}, u32[]{:S(2)}, u32[]{:S(2)}) collective-permute-start(bf16[256,768]{1,0:T(8,128)(2,1)S(1)} %get-tuple-element.82), channel_id=1, source_target_pairs={{4,0},{8,4},{12,8},{5,1},{9,5},{13,9},{6,2},{10,6},{14,10},{7,3},{... | collective-permute-start | bytes 1179656 | tf_op jit(solution)/shard_map/ppermute | solution.py:111
  314.6 19.8 %copy-start.13 = (bf16[1,4,256,768]{3,2,1,0:T(8,128)(2,1)S(1)}, bf16[1,4,256,768]{3,2,1,0:T(8,128)(2,1)}, u32[]{:S(2)}) copy-start(bf16[1,4,256,768]{3,2,1,0:T(8,128)(2,1)} %param.14) | copy-start | bytes 4718596
  314.6 19.8 %copy-start.22 = (f32[256,768]{1,0:T(8,128)S(1)}, f32[256,768]{1,0:T(8,128)}, u32[]{:S(2)}) copy-start(f32[256,768]{1,0:T(8,128)} %get-tuple-element.100) | copy-start | bytes 2359300
  334.3 4.5 copy-start.35
  334.4 10.7 %slice-start.6 = ((s8[9437184]{0:T(1024)(128)(4,1)}), s8[1048576]{0:T(1024)(128)(4,1)S(1)}, s32[]{:S(2)}) async-start(s8[9437184]{0:T(1024)(128)(4,1)} %bitcast.377), calls=%async_computation.13 | async-start | bytes 2097152
  334.8 3.9 collective-permute-start.7
  338.8 8.0 %copy-start.16 = (bf16[256,768]{1,0:T(8,128)(2,1)}, bf16[256,768]{1,0:T(8,128)(2,1)S(1)}, u32[]{:S(2)}) copy-start(bf16[256,768]{1,0:T(8,128)(2,1)S(1)} %get-tuple-element.71) | copy-start | bytes 1179652
  338.8 6.3 slice-start.7
  338.9 6.3 slice-start.8
  347.1 46.1 %copy-start.8 = (f32[256,768]{1,0:T(8,128)}, f32[256,768]{1,0:T(8,128)S(1)}, u32[]{:S(2)}) copy-start(f32[256,768]{1,0:T(8,128)S(1)} %get-tuple-element.73) | copy-start | bytes 2359300
  352.3 11.5 %copy-start.33 = (bf16[4,3,64,768]{3,2,1,0:T(8,128)(2,1)}, bf16[4,3,64,768]{3,2,1,0:T(8,128)(2,1)S(1)}, u32[]{:S(2)}) copy-start(bf16[4,3,64,768]{3,2,1,0:T(8,128)(2,1)S(1)} %get-tuple-element.113) | copy-start | bytes 3538948
  358.5 5.4 slice-start.18
  359.4 4.4 copy-start.19
  359.4 4.4 slice-start.19
  363.9 29.3 %slice-start.9 = ((s8[9437184]{0:T(1024)(128)(4,1)}), s8[4194304]{0:T(1024)(128)(4,1)S(1)}, s32[]{:S(2)}) async-start(s8[9437184]{0:T(1024)(128)(4,1)} %bitcast.380), calls=%async_computation.16 | async-start | bytes 8388608
  363.9 29.3 %slice-start.10 = ((s8[9437184]{0:T(1024)(128)(4,1)}), s8[4194304]{0:T(1024)(128)(4,1)S(1)}, s32[]{:S(2)}) async-start(s8[9437184]{0:T(1024)(128)(4,1)} %bitcast.380), calls=%async_computation.17 | async-start | bytes 8388608
  365.5 26.8 %collective-permute-start.9 = (bf16[256,768]{1,0:T(8,128)(2,1)S(1)}, bf16[256,768]{1,0:T(8,128)(2,1)S(1)}, u32[]{:S(2)}, u32[]{:S(2)}) collective-permute-start(bf16[256,768]{1,0:T(8,128)(2,1)S(1)} %get-tuple-element.81), channel_id=1, source_target_pairs={{8,0},{12,4},{9,1},{13,5},{10,2},{14,6},{11,3},{15,7},{24,16},{28,... | collective-permute-start | bytes 1179656 | tf_op jit(solution)/shard_map/ppermute | solution.py:111
  367.0 26.2 %slice-start.11 = ((s8[9437184]{0:T(1024)(128)(4,1)}), s8[1048576]{0:T(1024)(128)(4,1)S(1)}, s32[]{:S(2)}) async-start(s8[9437184]{0:T(1024)(128)(4,1)} %bitcast.380), calls=%async_computation.18 | async-start | bytes 2097152
  367.0 25.2 %collective-permute-start.8 = (bf16[256,768]{1,0:T(8,128)(2,1)S(1)}, bf16[256,768]{1,0:T(8,128)(2,1)S(1)}, u32[]{:S(2)}, u32[]{:S(2)}) collective-permute-start(bf16[256,768]{1,0:T(8,128)(2,1)S(1)} %get-tuple-element.80), channel_id=1, source_target_pairs={{4,0},{8,4},{12,8},{5,1},{9,5},{13,9},{6,2},{10,6},{14,10},{7,3},{... | collective-permute-start | bytes 1179656 | tf_op jit(solution)/shard_map/ppermute | solution.py:111
  370.1 23.1 %copy-start.7 = (f32[256,768]{1,0:T(8,128)S(1)}, f32[256,768]{1,0:T(8,128)}, u32[]{:S(2)}) copy-start(f32[256,768]{1,0:T(8,128)} %copy-done.6) | copy-start | bytes 2359300
  370.1 23.1 %copy-start.36 = (f32[4,768,256]{2,1,0:T(8,128)S(1)}, f32[4,768,256]{2,1,0:T(8,128)}, u32[]{:S(2)}) copy-start(f32[4,768,256]{2,1,0:T(8,128)} %fusion.37) | copy-start | bytes 9437188
  393.3 3.6 copy-start.11
  393.3 4.1 copy-start.24
  396.8 179.1 %reduce-scatter.3.cloned.1.call-start = ((), (), s32[]{:S(2)}) async-start(), calls=%async_computation.4 | async-start | bytes 5013504 | tf_op jit(solution)/shard_map/reduce_scatter | solution.py:267
  410.4 2.8 copy-start.17
  410.4 342.2 %reduce-scatter.5.cloned.1.call-start = ((), (), s32[]{:S(2)}) async-start(), calls=%async_computation.5 | async-start | bytes 10027008 | tf_op jit(solution)/shard_map/reduce_scatter | solution.py:264
  575.9 2.4 copy-start.9
  577.2 177.7 %copy-start.1 = (s32[4,1024]{1,0:T(4,128)S(1)}, s32[4,1024]{1,0:T(4,128)}, u32[]{:S(2)}) copy-start(s32[4,1024]{1,0:T(4,128)} %param.15) | copy-start | bytes 49156
  (9 other events, 13.9 us)
Sparse Core Ops, SparseCore 0:
  11.5 93.1 all-gather.6
  108.0 121.1 all-gather.8
  396.9 36.2 all-gather.10
  438.2 137.6 reduce-scatter.2
  582.4 170.2 reduce-scatter.4
